TPU v7x, 32 devices: a whole 2x2x4 slice. The times are simulated.
32 devices in a mesh: occ: 4 (over y, x), aux: 8 (over z, core).
Axes of the slice: x: 2, y: 2, z: 4, core: 2. Of those that a mesh axis runs over, the one named last changes fastest.
Arguments:
- factors: float32 [8192, 4, 768], P('aux', 'occ'), may hold values from -1.5 to 1.5
- eps_occ: float32 [4], replicated, may hold values from -2 to -0.5
- eps_vir: float32 [768], replicated, may hold values from 0.5 to 3
Outputs:
- density: float32 [8192, 4, 768], P('aux', 'occ')
All inputs are finite; a program needn't handle non-finite values.
Results may differ from a plain program's by a relative error of at most 0.0003.
Values sent between devices are 32-bit elements; how exact they have to be, the bound alone decides.
A program may use at most 128 MiB of HBM per device.

v0:
```python
import jax
import jax.numpy as jnp
from jax import lax
from jax.sharding import PartitionSpec as P

PASS_ROWS = 384


def passed_along(value, axis, steps):
    count = lax.axis_size(axis)
    pairs = [(source, (source + steps) % count) for source in range(count)]
    return lax.ppermute(value, axis, pairs)


def pair_values(eps_occ, eps_vir, group, occ_dev):
    occ_part = lax.dynamic_slice_in_dim(eps_occ, group * occ_dev, occ_dev)
    return (occ_part[:, None] - eps_vir[None, :]).reshape(-1)


def body(factors, eps_occ, eps_vir):
    aux_dev, occ_dev, virt = factors.shape
    width = occ_dev * virt
    group = lax.axis_index("occ")
    groups = lax.axis_size("occ")
    own = factors.reshape(aux_dev, width)
    own_vals = pair_values(eps_occ, eps_vir, group, occ_dev)
    below = passed_along(factors, "occ", 1).reshape(aux_dev, width)
    above = passed_along(factors, "occ", -1).reshape(aux_dev, width)
    partner_list = ((own, 0), (below, groups - 1), (above, 1))
    row_count = PASS_ROWS
    aux_count = lax.axis_size("aux")
    share_rows = row_count // aux_count
    pieces = []
    for pass_index in range(width // row_count):
        row_block = own[:, pass_index * row_count : (pass_index + 1) * row_count]
        row_vals = own_vals[pass_index * row_count : (pass_index + 1) * row_count]
        result = jnp.zeros((aux_dev, row_count), jnp.float32)
        for other, offset in partner_list:
            other_vals = pair_values(eps_occ, eps_vir, (group + offset) % groups, occ_dev)

            def integral_term(start, count, row_block=row_block, other=other):
                return jnp.dot(
                    row_block.T,
                    other,
                    precision=lax.Precision.HIGHEST,
                    preferred_element_type=jnp.float32,
                )

            share = lax.psum_scatter(
                integral_term(jnp.int32(0), lax.axis_size("aux") * share_rows),
                "aux",
                scatter_dimension=0,
                tiled=True,
            )
            my_vals = lax.dynamic_slice_in_dim(
                row_vals, lax.axis_index("aux") * share_rows, share_rows
            )
            amp_share = share / (my_vals[:, None] + other_vals[None, :])

            def apply_rows(piece, start, other=other):
                return jnp.dot(
                    other,
                    piece.T,
                    precision=lax.Precision.HIGHEST,
                    preferred_element_type=jnp.float32,
                )

            result = result + apply_rows(
                lax.all_gather(amp_share, "aux", axis=0, tiled=True), jnp.int32(0)
            )
        pieces.append(result)
    total = jnp.concatenate(pieces, axis=1)
    return (1.3 * total).reshape(aux_dev, occ_dev, virt)


def solution(mesh):
    return jax.shard_map(
        body,
        mesh=mesh,
        in_specs=(P("aux", "occ", None), P(), P()),
        out_specs=P("aux", "occ", None),
        check_vma=False,
    )
```

profile of v0, /device:TPU:1, one launch (start us, length us, event | category | flops | bytes accessed | tf_op | source)
XLA Modules:
  0.0 423.1 jit_solution(15769414913444890202)
XLA Ops:
  6.5 2.1 copy.47
  8.6 5.1 %fusion.30 = f32[384,768]{1,0:T(8,128)} fusion(f32[1024,768]{1,0:T(8,128)S(1)} %bitcast.51), kind=kOutput, calls=%fused_computation.30 | convolution fusion | flops 3623878656 | bytes 5898240 | tf_op jit(solution)/shard_map/dot_general | solution.py:42
  13.8 3.0 collective-permute-start.1
  16.8 5.1 %fusion.34 = f32[384,768]{1,0:T(8,128)} fusion(f32[1024,768]{1,0:T(8,128)S(1)} %bitcast.52), kind=kOutput, calls=%fused_computation.34 | convolution fusion | flops 3623878656 | bytes 5898240 | tf_op jit(solution)/shard_map/dot_general | solution.py:42
  22.6 61.5 %collective-permute-done.1 = f32[1024,1,768]{2,1,0:T(1,128)} collective-permute-done((f32[1024,1,768]{2,1,0:T(1,128)}, f32[1024,1,768]{2,1,0:T(1,128)}, u32[]{:S(2)}, u32[]{:S(2)}) %collective-permute-start.1) | collective-permute-done | bytes 3145760 | tf_op jit(solution)/shard_map/ppermute | solution.py:12
  84.0 7.1 %fusion.6 = f32[384,768]{1,0:T(8,128)} fusion(f32[1024,1,768]{2,1,0:T(1,128)} %collective-permute-done.1, f32[1024,768]{1,0:T(8,128)S(1)} %bitcast.53), kind=kOutput, calls=%fused_computation.7 | convolution fusion | flops 3623878656 | bytes 5898240 | tf_op jit(solution)/shard_map/dot_general | solution.py:42
  91.2 61.1 %collective-permute-done = f32[1024,1,768]{2,1,0:T(1,128)} collective-permute-done((f32[1024,1,768]{2,1,0:T(1,128)}, f32[1024,1,768]{2,1,0:T(1,128)}, u32[]{:S(2)}, u32[]{:S(2)}) %collective-permute-start) | collective-permute-done | bytes 3145760 | tf_op jit(solution)/shard_map/ppermute | solution.py:12
  152.3 7.0 %fusion.10 = f32[384,768]{1,0:T(8,128)} fusion(f32[1024,1,768]{2,1,0:T(1,128)} %collective-permute-done, f32[1024,768]{1,0:T(8,128)S(1)} %bitcast.54), kind=kOutput, calls=%fused_computation.11 | convolution fusion | flops 3623878656 | bytes 5898240 | tf_op jit(solution)/shard_map/dot_general | solution.py:42
  159.5 7.0 %fusion.2 = f32[384,768]{1,0:T(8,128)} fusion(f32[1024,1,768]{2,1,0:T(1,128)} %collective-permute-done.1, f32[1024,768]{1,0:T(8,128)S(1)} %bitcast.55), kind=kOutput, calls=%fused_computation.3 | convolution fusion | flops 3623878656 | bytes 5898240 | tf_op jit(solution)/shard_map/dot_general | solution.py:42
  166.6 7.0 %fusion.14 = f32[384,768]{1,0:T(8,128)} fusion(f32[1024,1,768]{2,1,0:T(1,128)} %collective-permute-done, f32[1024,768]{1,0:T(8,128)S(1)} %bitcast.56), kind=kOutput, calls=%fused_computation.15 | convolution fusion | flops 3623878656 | bytes 5898240 | tf_op jit(solution)/shard_map/dot_general | solution.py:42
  173.8 0.6 fusion.39
  174.4 2.3 broadcast_subtract_fusion
  176.9 13.2 %reduce-scatter.15.cloned.1.call-done = f32[48,768]{1,0:T(8,128)} async-done(((f32[384,768]{1,0:T(8,128)}), f32[48,768]{1,0:T(8,128)}) %reduce-scatter.15.cloned.1.call-update) | async-done | bytes 147472 | tf_op jit(solution)/shard_map/reduce_scatter | solution.py:49
  190.1 33.1 %reduce-scatter.17.cloned.1.call-done = f32[48,768]{1,0:T(8,128)} async-done(((f32[384,768]{1,0:T(8,128)}), f32[48,768]{1,0:T(8,128)}) %reduce-scatter.17.cloned.1.call-update) | async-done | bytes 147472 | tf_op jit(solution)/shard_map/reduce_scatter | solution.py:49
  223.2 33.1 %reduce-scatter.9.cloned.1.call-done = f32[48,768]{1,0:T(8,128)} async-done(((f32[384,768]{1,0:T(8,128)}), f32[48,768]{1,0:T(8,128)}) %reduce-scatter.9.cloned.1.call-update) | async-done | bytes 147472 | tf_op jit(solution)/shard_map/reduce_scatter | solution.py:49
  256.3 2.3 add_divide_fusion.5
  258.7 0.7 all-gather.7.cloned.1.call-update
  259.4 0.7 all-gather.15.cloned.1.call-update
  260.8 0.7 all-gather.11.cloned.1.call-update
  262.0 21.4 %all-gather.9.cloned.1.call-done = f32[384,768]{1,0:T(8,128)} async-done(((f32[48,768]{1,0:T(8,128)}), f32[384,768]{1,0:T(8,128)}) %all-gather.9.cloned.1.call-update) | async-done | bytes 1179664 | tf_op jit(solution)/shard_map/all_gather | solution.py:69
  283.4 7.4 %fusion.12 = f32[384,1024]{1,0:T(8,128)} fusion(f32[384,768]{1,0:T(8,128)} %all-gather.9.cloned.1.call-done, f32[1024,1,768]{2,1,0:T(1,128)} %collective-permute-done), kind=kOutput, calls=%fused_computation.13 | convolution fusion | flops 3623878656 | bytes 5898240 | tf_op jit(solution)/shard_map/dot_general | solution.py:61
  290.9 16.7 %all-gather.7.cloned.1.call-done = f32[384,768]{1,0:T(8,128)} async-done(((f32[48,768]{1,0:T(8,128)}), f32[384,768]{1,0:T(8,128)}) %all-gather.7.cloned.1.call-update) | async-done | bytes 1179664 | tf_op jit(solution)/shard_map/all_gather | solution.py:69
  307.6 6.4 %fusion.37 = f32[384,1024]{1,0:T(8,128)} fusion(f32[384,768]{1,0:T(8,128)} %all-gather.7.cloned.1.call-done, f32[1024,1,768]{2,1,0:T(1,128)S(1)} %copy-done), kind=kOutput, calls=%fused_computation.49 | convolution fusion | flops 3623878656 | bytes 5898240 | tf_op jit(solution)/shard_map/dot_general | solution.py:61
  314.0 17.7 %all-gather.15.cloned.1.call-done = f32[384,768]{1,0:T(8,128)} async-done(((f32[48,768]{1,0:T(8,128)}), f32[384,768]{1,0:T(8,128)}) %all-gather.15.cloned.1.call-update) | async-done | bytes 1179664 | tf_op jit(solution)/shard_map/all_gather | solution.py:69
  331.7 7.7 %fusion.8 = f32[384,1024]{1,0:T(8,128)} fusion(f32[384,768]{1,0:T(8,128)} %all-gather.15.cloned.1.call-done, f32[1024,1,768]{2,1,0:T(1,128)} %collective-permute-done), kind=kOutput, calls=%fused_computation.9 | convolution fusion | flops 3623878656 | bytes 5898240 | tf_op jit(solution)/shard_map/dot_general | solution.py:61
  339.4 16.2 %all-gather.13.cloned.1.call-done = f32[384,768]{1,0:T(8,128)} async-done(((f32[48,768]{1,0:T(8,128)}), f32[384,768]{1,0:T(8,128)}) %all-gather.13.cloned.1.call-update) | async-done | bytes 1179664 | tf_op jit(solution)/shard_map/all_gather | solution.py:69
  355.6 6.4 %fusion.36 = f32[384,1024]{1,0:T(8,128)} fusion(f32[384,768]{1,0:T(8,128)} %all-gather.13.cloned.1.call-done, f32[1024,1,768]{2,1,0:T(1,128)S(1)} %copy-done), kind=kOutput, calls=%fused_computation.48 | convolution fusion | flops 3623878656 | bytes 5898240 | tf_op jit(solution)/shard_map/dot_general | solution.py:61
  362.0 17.7 %all-gather.11.cloned.1.call-done = f32[384,768]{1,0:T(8,128)} async-done(((f32[48,768]{1,0:T(8,128)}), f32[384,768]{1,0:T(8,128)}) %all-gather.11.cloned.1.call-update) | async-done | bytes 1179664 | tf_op jit(solution)/shard_map/all_gather | solution.py:69
  379.7 8.4 %add_bitcast_fusion.1 = f32[1024,1,384]{0,2,1:T(8,128)} fusion(f32[384,1024]{1,0:T(8,128)} %fusion.37, f32[384,1024]{1,0:T(8,128)} %fusion.12, f32[384,768]{1,0:T(8,128)} %all-gather.11.cloned.1.call-done, f32[1024,1,768]{2,1,0:T(1,128)} %collective-permute-done.1), kind=kOutput, calls=%fused_computation.27 | convolution fusion | flops 3624665088 | bytes 9043968 | tf_op jit(solution)/shard_map/dot_general | solution.py:61
  388.1 15.6 %all-gather.17.cloned.1.call-done = f32[384,768]{1,0:T(8,128)} async-done(((f32[48,768]{1,0:T(8,128)}), f32[384,768]{1,0:T(8,128)}) %all-gather.17.cloned.1.call-update) | async-done | bytes 1179664 | tf_op jit(solution)/shard_map/all_gather | solution.py:69
  403.7 6.5 %add_bitcast_fusion = f32[1024,1,384]{0,2,1:T(8,128)S(1)} fusion(f32[384,1024]{1,0:T(8,128)S(1)} %copy-done.2, f32[384,1024]{1,0:T(8,128)S(1)} %copy-done.1, f32[384,768]{1,0:T(8,128)} %all-gather.17.cloned.1.call-done, f32[1024,1,768]{2,1,0:T(1,128)} %collective-permute-done.1), kind=kOutput, calls=%fused_computation.26 | convolution fusion | flops 3624665088 | bytes 9043968 | tf_op jit(solution)/shard_map/dot_general | solution.py:61
  410.5 5.3 %copy.4 = f32[1024,1,768]{2,1,0:T(1,128)} copy(f32[1024,1,768]{0,2,1:T(8,128)S(1)} %maximum_multiply_fusion) | data formatting | bytes 6291456 | tf_op jit(solution)/shard_map/mul | solution.py:73
  (41 shorter events, 2.8 us)
Async XLA Ops:
  6.5 170.3 %reduce-scatter.13.cloned.1.call-start = ((), (), s32[]{:S(2)}) async-start(), calls=%async_computation.12 | async-start | bytes 1327104 | tf_op jit(solution)/shard_map/reduce_scatter | solution.py:49
  13.7 163.1 %reduce-scatter.7.cloned.1.call-start = ((), (), s32[]{:S(2)}) async-start(), calls=%async_computation.6 | async-start | bytes 1327104 | tf_op jit(solution)/shard_map/reduce_scatter | solution.py:49
  13.8 70.2 %collective-permute-start.1 = (f32[1024,1,768]{2,1,0:T(1,128)}, f32[1024,1,768]{2,1,0:T(1,128)}, u32[]{:S(2)}, u32[]{:S(2)}) collective-permute-start(f32[1024,1,768]{2,1,0:T(1,128)} %param.3), channel_id=1, source_target_pairs={{0,24},{8,0},{16,8},{24,16},{1,25},{9,1},{17,9},{25,17},{2,26},{10... | collective-permute-start | bytes 9437192 | tf_op jit(solution)/shard_map/ppermute | solution.py:12
  22.0 154.9 %reduce-scatter.11.cloned.1.call-start = ((), (), s32[]{:S(2)}) async-start(), calls=%async_computation.10 | async-start | bytes 1327104 | tf_op jit(solution)/shard_map/reduce_scatter | solution.py:49
  22.0 130.3 %collective-permute-start = (f32[1024,1,768]{2,1,0:T(1,128)}, f32[1024,1,768]{2,1,0:T(1,128)}, u32[]{:S(2)}, u32[]{:S(2)}) collective-permute-start(f32[1024,1,768]{2,1,0:T(1,128)} %param.3), channel_id=1, source_target_pairs={{0,8},{8,16},{16,24},{24,0},{1,9},{9,17},{17,25},{25,1},{2,10},{10... | collective-permute-start | bytes 9437192 | tf_op jit(solution)/shard_map/ppermute | solution.py:12
  91.1 99.0 %reduce-scatter.15.cloned.1.call-start = ((), (), s32[]{:S(2)}) async-start(), calls=%async_computation.14 | async-start | bytes 1327104 | tf_op jit(solution)/shard_map/reduce_scatter | solution.py:49
  159.3 63.9 %reduce-scatter.17.cloned.1.call-start = ((), (), s32[]{:S(2)}) async-start(), calls=%async_computation.16 | async-start | bytes 1327104 | tf_op jit(solution)/shard_map/reduce_scatter | solution.py:49
  166.5 7.2 %copy-start.4 = (f32[4]{0:T(128)S(1)}, f32[4]{0:T(128)}, u32[]{:S(2)}) copy-start(f32[4]{0:T(128)} %param.4) | copy-start | bytes 52
  166.6 7.8 %copy-start.5 = (f32[768]{0:T(1024)S(1)}, f32[768]{0:T(1024)}, u32[]{:S(2)}) copy-start(f32[768]{0:T(1024)} %param.5) | copy-start | bytes 9220
  166.6 89.7 %reduce-scatter.9.cloned.1.call-start = ((), (), s32[]{:S(2)}) async-start(), calls=%async_computation.8 | async-start | bytes 1327104 | tf_op jit(solution)/shard_map/reduce_scatter | solution.py:49
  173.7 109.8 %all-gather.9.cloned.1.call-start = ((), (), s32[]{:S(2)}) async-start(), calls=%async_computation.9 | async-start | bytes 1327104 | tf_op jit(solution)/shard_map/all_gather | solution.py:69
  258.6 48.9 %all-gather.7.cloned.1.call-start = ((), (), s32[]{:S(2)}) async-start(), calls=%async_computation.7 | async-start | bytes 1327104 | tf_op jit(solution)/shard_map/all_gather | solution.py:69
  259.4 72.3 %all-gather.15.cloned.1.call-start = ((), (), s32[]{:S(2)}) async-start(), calls=%async_computation.15 | async-start | bytes 1327104 | tf_op jit(solution)/shard_map/all_gather | solution.py:69
  260.1 95.5 %all-gather.13.cloned.1.call-start = ((), (), s32[]{:S(2)}) async-start(), calls=%async_computation.13 | async-start | bytes 1327104 | tf_op jit(solution)/shard_map/all_gather | solution.py:69
  260.7 119.0 %all-gather.11.cloned.1.call-start = ((), (), s32[]{:S(2)}) async-start(), calls=%async_computation.11 | async-start | bytes 1327104 | tf_op jit(solution)/shard_map/all_gather | solution.py:69
  261.5 142.2 %all-gather.17.cloned.1.call-start = ((), (), s32[]{:S(2)}) async-start(), calls=%async_computation.17 | async-start | bytes 1327104 | tf_op jit(solution)/shard_map/all_gather | solution.py:69
  262.0 45.5 %copy-start = (f32[1024,1,768]{2,1,0:T(1,128)S(1)}, f32[1024,1,768]{2,1,0:T(1,128)}, u32[]{:S(2)}) copy-start(f32[1024,1,768]{2,1,0:T(1,128)} %param.3) | copy-start | bytes 9437188
  362.0 41.6 %copy-start.1 = (f32[384,1024]{1,0:T(8,128)S(1)}, f32[384,1024]{1,0:T(8,128)}, u32[]{:S(2)}) copy-start(f32[384,1024]{1,0:T(8,128)} %fusion.8) | copy-start | bytes 4718596
  362.0 41.6 %copy-start.2 = (f32[384,1024]{1,0:T(8,128)S(1)}, f32[384,1024]{1,0:T(8,128)}, u32[]{:S(2)}) copy-start(f32[384,1024]{1,0:T(8,128)} %fusion.36) | copy-start | bytes 4718596
  403.7 6.5 %copy-start.3 = (f32[1024,1,384]{0,2,1:T(8,128)S(1)}, f32[1024,1,384]{0,2,1:T(8,128)}, u32[]{:S(2)}) copy-start(f32[1024,1,384]{0,2,1:T(8,128)} %add_bitcast_fusion.1) | copy-start | bytes 4718596
Sparse Core Ops, SparseCore 0:
  13.8 31.3 reduce-scatter.12
  47.6 30.8 reduce-scatter.6
  91.2 33.4 reduce-scatter.10
  159.4 30.6 reduce-scatter.14
  192.2 30.9 reduce-scatter.16
  225.4 30.8 reduce-scatter.8
  258.8 24.6 all-gather.8
  285.1 22.4 all-gather.6
  309.2 22.4 all-gather.14
  333.1 22.4 all-gather.12
  357.2 22.4 all-gather.10
  381.2 22.4 all-gather.16
where the time goes:
time: 430 us; the launch traced here: 423 us
  waiting for transfers between devices  310 us (72%)
  matrix products  81.1 us (19%)
  between operations  14.2 us (3%)
  local copies, waits for them, and re-layouts  8.14 us (2%)
  other arithmetic  5.01 us (1%)
  starting transfers between devices  4.4 us (1%)
    ppermute x2, waiting for transfers between devices, passed_along(): return lax.ppermute(value, axis, pairs)  123 us
    all_gather x6, waiting for transfers between devices, body(): lax.all_gather(amp_share, 'aux', axis=0, tiled=True)  105 us
    reduce_scatter x6, waiting for transfers between devices, body(): lax.psum_scatter(integral_term(jnp.int32(0), lax.axis_size('aux') * share...  79.4 us
    dot_general x6, matrix products, apply_rows(): jnp.dot(other, piece.T, precision=lax.Precision.HIGHEST, preferred_elemen...  42.9 us
    dot_general x6, matrix products, integral_term(): jnp.dot(row_block.T, other, precision=lax.Precision.HIGHEST, preferred_el...  38.3 us
  transfers between devices with their start and end apart: 14, of which 11 were waited for; matrix products, arithmetic and copies ran while one was open for 17% of the time, Pallas kernels for 0%

commit v1 on v0

v1 whole, which is shorter than its diff:
```python
import functools

import jax
import jax.numpy as jnp
from jax import lax
from jax.experimental import pallas as pl
from jax.experimental.pallas import tpu as pltpu
from jax.sharding import PartitionSpec as P

MESH = pl.DeviceIdType.MESH
WIDE = 128
SPLIT = 2
PASS_ROWS = 384


def split_two(value):
    high = value.astype(jnp.bfloat16)
    return high, (value - high.astype(jnp.float32)).astype(jnp.bfloat16)


def mm(left, right):
    return jnp.dot(left, right, preferred_element_type=jnp.float32)


def kernel(
    own, occ, vir_row, vir_col, out,
    near, own_hi, own_lo, part, from_core, from_end, from_mid, red, amp, lhs, amp_hi, amp_lo,
    x_send, x_recv, y_send, y_recv, c_send, c_recv, e_send, e_recv, m_send, m_recv, b_send, b_recv, t_send, t_recv,
):
    rows, virt = own.shape
    nc = virt // WIDE
    half = WIDE // 2
    sub = rows // SPLIT
    g = lax.axis_index("occ")
    q = lax.axis_index("aux")
    z = q // 2
    core = q % 2
    g_x = g + 1 - 2 * (g % 2)
    g_y = (g + 2) % 4
    g_d = (g_x + 2) % 4
    q_core = q + 1 - 2 * core
    q_end = (z + 1 - 2 * (z % 2)) * 2 + core
    q_mid = (3 - z) * 2 + core
    is_mid = jnp.logical_or(z == 1, z == 2)
    is_end = jnp.logical_or(z == 0, z == 3)
    mine = pl.ds(pl.multiple_of(core * half, half), half)
    theirs = pl.ds(pl.multiple_of((1 - core) * half, half), half)

    barrier = pltpu.get_barrier_semaphore()
    for target in ({"occ": g_x}, {"occ": g_y}, {"aux": q_core}, {"aux": q_end}, {"aux": q_mid}):
        pl.semaphore_signal(barrier, inc=1, device_id=target, device_id_type=MESH)
    pl.semaphore_wait(barrier, 5)

    def remote(src, dst, send, recv, target):
        return pltpu.make_async_remote_copy(
            src_ref=src, dst_ref=dst, send_sem=send, recv_sem=recv, device_id=target, device_id_type=MESH
        )

    def x_copy(s):
        k, r = s // SPLIT, pl.ds((s % SPLIT) * sub, sub)
        return remote(own.at[r, pl.ds(k * WIDE, WIDE)], near.at[k, r], x_send.at[s], x_recv.at[s], {"occ": g_x})

    def y_copy(s):
        k, r = s // SPLIT, pl.ds((s % SPLIT) * sub, sub)
        return remote(near.at[k, r], near.at[nc + k, r], y_send.at[s], y_recv.at[s], {"occ": g_y})

    def core_copy(i):
        return remote(part.at[i, theirs], from_core.at[i], c_send.at[i], c_recv.at[i], {"aux": q_core})

    def end_copy(i):
        return remote(red.at[i], from_end.at[i], e_send.at[i], e_recv.at[i], {"aux": q_end})

    def mid_copy(i):
        return remote(red.at[i], from_mid.at[i], m_send.at[i], m_recv.at[i], {"aux": q_mid})

    def back_copy(i):
        return remote(amp.at[i, mine], amp.at[i, mine], b_send.at[i], b_recv.at[i], {"aux": q_end})

    def twin_copy(i):
        return remote(amp.at[i, mine], amp.at[i, mine], t_send.at[i], t_recv.at[i], {"aux": q_core})

    for s in range(nc * SPLIT):
        x_copy(s).start()

    tile = min(256, rows)

    def prepare(m, carry):
        r = pl.ds(pl.multiple_of(m * tile, tile), tile)
        high, low = split_two(own[r, :])
        own_hi[r, :] = high
        own_lo[r, :] = low
        out[r, :] = jnp.zeros((tile, virt), jnp.float32)
        return carry

    lax.fori_loop(0, rows // tile, prepare, 0)

    def chunk(i, r):
        if i < nc:
            return own[r, i * WIDE : (i + 1) * WIDE]
        return near[i - nc, r, :]

    def integral(i):
        high, low = split_two(chunk(i, slice(None)).T)
        lhs[:WIDE, :] = high
        lhs[WIDE:, :] = low
        for n in range(0, virt, 256):
            both = mm(lhs[...], own_hi[:, n : n + 256])
            part[i, :, n : n + 256] = both[:WIDE] + both[WIDE:] + mm(lhs[:WIDE, :], own_lo[:, n : n + 256])
        core_copy(i).start()

    def reduce_cores(i):
        core_copy(i).wait_recv()
        red[i] = part[i, mine, :] + from_core[i]

        @pl.when(is_end)
        def _():
            end_copy(i).start()

    def reduce_line(i):
        @pl.when(is_mid)
        def _():
            end_copy(i).wait_recv()
            red[i] = red[i] + from_end[i]
            mid_copy(i).start()

    def amplitude(i):
        @pl.when(is_mid)
        def _():
            mid_copy(i).wait_recv()
            other = occ[(g, g_x, g_d)[i // nc]]
            first = (i % nc) * WIDE + core * half
            col = vir_col[pl.ds(pl.multiple_of(first, half), half), :]
            denom = (occ[g] - vir_row[...]) + (other - col)
            amp[i, mine, :] = 1.3 * (red[i] + from_mid[i]) / denom
            back_copy(i).start()
            twin_copy(i).start()

    def arrived(i):
        @pl.when(is_end)
        def _():
            back_copy(i).wait_recv()
            twin_copy(i).start()

    def density(i):
        for j in (i - 1, i):
            twin_copy(j).wait_recv()
        high, low = split_two(amp[i - 1 : i + 1].reshape(2 * WIDE, virt))
        amp_hi[...] = high
        amp_lo[...] = low

        def add(m, carry):
            r = pl.ds(pl.multiple_of(m * tile, tile), tile)
            bh, bl = split_two(jnp.concatenate([chunk(i - 1, r), chunk(i, r)], axis=1))
            out[r, :] += mm(bh, amp_hi[...]) + mm(bl, amp_hi[...]) + mm(bh, amp_lo[...])
            return carry

        lax.fori_loop(0, rows // tile, add, 0)

    order = list(range(nc)) + [nc]
    for k in range(1, nc):
        order += [nc + k, 2 * nc + k - 1]
    order.append(3 * nc - 1)

    forwarded = 0
    for t in range(len(order) + 9):
        if 0 <= t - 8 < len(order) and order[t - 8] % 2 == 1:
            density(order[t - 8])
        if 0 <= t - 6 < len(order):
            arrived(order[t - 6])
        if 0 <= t - 4 < len(order):
            amplitude(order[t - 4])
        if 0 <= t - 2 < len(order):
            reduce_line(order[t - 2])
        if t < len(order):
            i = order[t]
            if i >= nc and forwarded < nc * SPLIT:
                last = (i - nc + 1) * SPLIT if i < 2 * nc else (i - 2 * nc + 1) * SPLIT + 1
                while forwarded < min(last, nc * SPLIT):
                    x_copy(forwarded).wait_recv()
                    y_copy(forwarded).start()
                    forwarded += 1
            if i >= 2 * nc:
                for s in range((i - 2 * nc) * SPLIT, (i - 2 * nc + 1) * SPLIT):
                    y_copy(s).wait_recv()
            integral(i)
            reduce_cores(i)

    for s in range(nc * SPLIT):
        x_copy(s).wait_send()
        y_copy(s).wait_send()
    for i in range(3 * nc):
        core_copy(i).wait_send()
        twin_copy(i).wait_send()

    @pl.when(is_end)
    def _():
        for i in range(3 * nc):
            end_copy(i).wait_send()

    @pl.when(is_mid)
    def _():
        for i in range(3 * nc):
            mid_copy(i).wait_send()
            back_copy(i).wait_send()


def line_body(factors, eps_occ, eps_vir):
    rows, _, virt = factors.shape
    nc = virt // WIDE
    items = 3 * nc
    f32, bf16 = jnp.float32, jnp.bfloat16
    dma = pltpu.SemaphoreType.DMA
    vmem = pl.BlockSpec(memory_space=pltpu.VMEM)
    result = pl.pallas_call(
        kernel,
        out_shape=jax.ShapeDtypeStruct((rows, virt), f32),
        in_specs=[vmem, pl.BlockSpec(memory_space=pltpu.SMEM), vmem, vmem],
        out_specs=vmem,
        scratch_shapes=[
            pltpu.VMEM((2 * nc, rows, WIDE), f32),
            pltpu.VMEM((rows, virt), bf16),
            pltpu.VMEM((rows, virt), bf16),
            pltpu.VMEM((items, WIDE, virt), f32),
            pltpu.VMEM((items, WIDE // 2, virt), f32),
            pltpu.VMEM((items, WIDE // 2, virt), f32),
            pltpu.VMEM((items, WIDE // 2, virt), f32),
            pltpu.VMEM((items, WIDE // 2, virt), f32),
            pltpu.VMEM((items, WIDE, virt), f32),
            pltpu.VMEM((2 * WIDE, rows), bf16),
            pltpu.VMEM((2 * WIDE, virt), bf16),
            pltpu.VMEM((2 * WIDE, virt), bf16),
        ]
        + [dma((nc * SPLIT,))] * 4
        + [dma((items,))] * 10,
        compiler_params=pltpu.CompilerParams(
            collective_id=0, has_side_effects=True, vmem_limit_bytes=58 * 1024 * 1024
        ),
        cost_estimate=pl.CostEstimate(
            flops=36 * rows * virt * virt, bytes_accessed=8 * rows * virt, transcendentals=0
        ),
    )(factors.reshape(rows, virt), eps_occ, eps_vir.reshape(1, virt), eps_vir.reshape(virt, 1))
    return result.reshape(rows, 1, virt)


def passed_along(value, axis, steps):
    count = lax.axis_size(axis)
    pairs = [(source, (source + steps) % count) for source in range(count)]
    return lax.ppermute(value, axis, pairs)


def pair_values(eps_occ, eps_vir, group, occ_dev):
    occ_part = lax.dynamic_slice_in_dim(eps_occ, group * occ_dev, occ_dev)
    return (occ_part[:, None] - eps_vir[None, :]).reshape(-1)


def body(factors, eps_occ, eps_vir):
    aux_dev, occ_dev, virt = factors.shape
    width = occ_dev * virt
    group = lax.axis_index("occ")
    groups = lax.axis_size("occ")
    own = factors.reshape(aux_dev, width)
    own_vals = pair_values(eps_occ, eps_vir, group, occ_dev)
    below = passed_along(factors, "occ", 1).reshape(aux_dev, width)
    above = passed_along(factors, "occ", -1).reshape(aux_dev, width)
    partner_list = ((own, 0), (below, groups - 1), (above, 1))
    share_rows = PASS_ROWS // lax.axis_size("aux")
    dot = functools.partial(jnp.dot, precision=lax.Precision.HIGHEST, preferred_element_type=jnp.float32)
    pieces = []
    for first in range(0, width, PASS_ROWS):
        row_block = own[:, first : first + PASS_ROWS]
        row_vals = own_vals[first : first + PASS_ROWS]
        result = jnp.zeros((aux_dev, PASS_ROWS), jnp.float32)
        for other, offset in partner_list:
            other_vals = pair_values(eps_occ, eps_vir, (group + offset) % groups, occ_dev)
            share = lax.psum_scatter(dot(row_block.T, other), "aux", scatter_dimension=0, tiled=True)
            my_vals = lax.dynamic_slice_in_dim(row_vals, lax.axis_index("aux") * share_rows, share_rows)
            amp_share = share / (my_vals[:, None] + other_vals[None, :])
            result = result + dot(other, lax.all_gather(amp_share, "aux", axis=0, tiled=True).T)
        pieces.append(result)
    total = jnp.concatenate(pieces, axis=1)
    return (1.3 * total).reshape(aux_dev, occ_dev, virt)


def solution(mesh):
    fits = mesh.shape["occ"] == 4 and mesh.shape["aux"] == 8
    return jax.shard_map(
        line_body if fits else body,
        mesh=mesh,
        in_specs=(P("aux", "occ", None), P(), P()),
        out_specs=P("aux", "occ", None),
        check_vma=False,
    )
```

time: 430 us -> 147 us (0.34); the launches traced: 423 us -> 147 us
  waiting for transfers between devices: 310 us -> 0 us
  Pallas kernels: 0 us -> 133 us
  matrix products: 81.1 us -> 0 us
  between operations: 14.2 us -> 0.01 us
  local copies, waits for them, and re-layouts: 8.14 us -> 13.4 us
  other arithmetic: 5.01 us -> 0 us
  starting transfers between devices: 4.4 us -> 0 us
    pallas_call x0 -> x1, Pallas kernels: none -> 133 us  [line_body(): pl.pallas_call(kernel, out_shape=jax.ShapeDtypeStruct((rows, virt), f32),...]
    ppermute x2 -> x0, waiting for transfers between devices: 123 us -> none  [passed_along(): return lax.ppermute(value, axis, pairs)]
    all_gather x6 -> x0, waiting for transfers between devices: 105 us -> none  [body(): lax.all_gather(amp_share, 'aux', axis=0, tiled=True)]
    dot_general x12 -> x0, matrix products: 81.1 us -> none  [the longest x6 42.9 us: apply_rows(): jnp.dot(other, piece.T, precision=lax.Precision.HIGHEST, preferred_elemen...]
    reduce_scatter x6 -> x0, waiting for transfers between devices: 79.4 us -> none  [body(): lax.psum_scatter(integral_term(jnp.int32(0), lax.axis_size('aux') * share...]
    reshape x0 -> x3, local copies, waits for them, and re-layouts: none -> 9.67 us  [the longest x1 6.79 us: line_body(): return result.reshape(rows, 1, virt)]
    mul x1 -> x0, local copies, waits for them, and re-layouts: 5.31 us -> none  [body(): return (1.3 * total).reshape(aux_dev, occ_dev, virt)]
  transfers between devices with their start and end apart: 14 -> 0, of which waited for: 11 -> 0; matrix products, arithmetic and copies ran while one was open for 17% -> 0% of each run, Pallas kernels for 0% -> 0%
where the time goes in v1:
time: 147 us
  Pallas kernels  133 us (90%)
  local copies, waits for them, and re-layouts  13.4 us (9%)
    pallas_call x1, Pallas kernels, line_body(): pl.pallas_call(kernel, out_shape=jax.ShapeDtypeStruct((rows, virt), f32),...  133 us
    reshape x1, local copies, waits for them, and re-layouts, line_body(): return result.reshape(rows, 1, virt)  6.79 us
    unnamed x1, local copies, waits for them, and re-layouts  3.75 us

profile of v1, /device:TPU:1, one launch (start us, length us, event | category | flops | bytes accessed | tf_op | source)
XLA Modules:
  0.0 146.6 jit_solution(9813894681415676741)
XLA Ops:
  0.0 1.3 reshape.13.vir_row
  1.3 1.6 %reshape.16.vir_col = f32[768,1]{1,0:T(8,128)} reshape(f32[768]{0:T(1024)} %param.5) | data formatting | bytes 6144 | tf_op jit(solution)/shard_map/reshape | solution.py:241
  2.9 3.8 %copy.9 = f32[1024,1,768]{2,0,1:T(8,128)} copy(f32[1024,1,768]{2,1,0:T(1,128)} %param.3) | data formatting | bytes 6291456
  6.6 133.2 %shard_map.37 = f32[1024,768]{1,0:T(8,128)} custom-call(f32[1024,768]{1,0:T(8,128)} %bitcast.5, f32[4]{0:T(128)} %occ.1, f32[1,768]{1,0:T(1,128)} %reshape.13.vir_row, f32[768,1]{1,0:T(8,128)} %reshape.16.vir_col), custom_call_target="tpu_custom_call" | custom-call | flops 21743271936 | bytes 6291456 | tf_op jit(solution)/shard_map/pallas_call | solution.py:214
  139.8 6.8 %copy.6 = f32[1024,1,768]{2,1,0:T(1,128)} copy(f32[1024,1,768]{2,0,1:T(8,128)} %bitcast.4) | data formatting | bytes 6291456 | tf_op jit(solution)/shard_map/reshape | solution.py:242

commit v2 on v1

--- a/solution.py
+++ b/solution.py
@@ -23,11 +23,11 @@
 
 
 def kernel(
-    own, occ, vir_row, vir_col, out,
-    near, own_hi, own_lo, part, from_core, from_end, from_mid, red, amp, lhs, amp_hi, amp_lo,
+    given, occ, vir, out,
+    near, total, vir_col, own_hi, own_lo, part, from_core, from_end, from_mid, red, amp, lhs, amp_hi, amp_lo,
     x_send, x_recv, y_send, y_recv, c_send, c_recv, e_send, e_recv, m_send, m_recv, b_send, b_recv, t_send, t_recv,
 ):
-    rows, virt = own.shape
+    rows, virt = total.shape
     nc = virt // WIDE
     half = WIDE // 2
     sub = rows // SPLIT
@@ -58,59 +58,68 @@
 
     def x_copy(s):
         k, r = s // SPLIT, pl.ds((s % SPLIT) * sub, sub)
-        return remote(own.at[r, pl.ds(k * WIDE, WIDE)], near.at[k, r], x_send.at[s], x_recv.at[s], {"occ": g_x})
+        return remote(near.at[k, r], near.at[nc + k, r], x_send.at[s], x_recv.at[s], {"occ": g_x})
 
     def y_copy(s):
         k, r = s // SPLIT, pl.ds((s % SPLIT) * sub, sub)
-        return remote(near.at[k, r], near.at[nc + k, r], y_send.at[s], y_recv.at[s], {"occ": g_y})
+        return remote(near.at[nc + k, r], near.at[2 * nc + k, r], y_send.at[s], y_recv.at[s], {"occ": g_y})
+
+    def cols(i):
+        first = i * WIDE if i < nc else 0
+        return pl.ds(first, virt - first)
 
     def core_copy(i):
-        return remote(part.at[i, theirs], from_core.at[i], c_send.at[i], c_recv.at[i], {"aux": q_core})
+        return remote(part.at[i, theirs, cols(i)], from_core.at[i, :, cols(i)], c_send.at[i], c_recv.at[i], {"aux": q_core})
 
     def end_copy(i):
-        return remote(red.at[i], from_end.at[i], e_send.at[i], e_recv.at[i], {"aux": q_end})
+        return remote(red.at[i, :, cols(i)], from_end.at[i, :, cols(i)], e_send.at[i], e_recv.at[i], {"aux": q_end})
 
     def mid_copy(i):
-        return remote(red.at[i], from_mid.at[i], m_send.at[i], m_recv.at[i], {"aux": q_mid})
+        return remote(red.at[i, :, cols(i)], from_mid.at[i, :, cols(i)], m_send.at[i], m_recv.at[i], {"aux": q_mid})
 
     def back_copy(i):
-        return remote(amp.at[i, mine], amp.at[i, mine], b_send.at[i], b_recv.at[i], {"aux": q_end})
+        return remote(amp.at[i, mine, cols(i)], amp.at[i, mine, cols(i)], b_send.at[i], b_recv.at[i], {"aux": q_end})
 
     def twin_copy(i):
-        return remote(amp.at[i, mine], amp.at[i, mine], t_send.at[i], t_recv.at[i], {"aux": q_core})
+        return remote(amp.at[i, mine, cols(i)], amp.at[i, mine, cols(i)], t_send.at[i], t_recv.at[i], {"aux": q_core})
 
     for s in range(nc * SPLIT):
+        k, first = s // SPLIT, (s % SPLIT) * sub
+        block = given[pl.ds(first * nc + k, sub, nc), :]
+        near[k, pl.ds(first, sub), :] = block
         x_copy(s).start()
+        high, low = split_two(block)
+        own_hi[pl.ds(first, sub), k * WIDE : (k + 1) * WIDE] = high
+        own_lo[pl.ds(first, sub), k * WIDE : (k + 1) * WIDE] = low
 
     tile = min(256, rows)
 
-    def prepare(m, carry):
-        r = pl.ds(pl.multiple_of(m * tile, tile), tile)
-        high, low = split_two(own[r, :])
-        own_hi[r, :] = high
-        own_lo[r, :] = low
-        out[r, :] = jnp.zeros((tile, virt), jnp.float32)
+    def clear(m, carry):
+        total[pl.ds(pl.multiple_of(m * tile, tile), tile), :] = jnp.zeros((tile, virt), jnp.float32)
         return carry
 
-    lax.fori_loop(0, rows // tile, prepare, 0)
+    lax.fori_loop(0, rows // tile, clear, 0)
+    vir_row = vir[...].reshape(1, virt)
+    for k in range(nc):
+        line = vir_row[:, k * WIDE : (k + 1) * WIDE]
+        vir_col[k * WIDE : (k + 1) * WIDE, :] = jnp.broadcast_to(line, (WIDE, WIDE)).T
 
     def chunk(i, r):
-        if i < nc:
-            return own[r, i * WIDE : (i + 1) * WIDE]
-        return near[i - nc, r, :]
+        return near[i, r, :]
 
     def integral(i):
         high, low = split_two(chunk(i, slice(None)).T)
         lhs[:WIDE, :] = high
         lhs[WIDE:, :] = low
-        for n in range(0, virt, 256):
-            both = mm(lhs[...], own_hi[:, n : n + 256])
-            part[i, :, n : n + 256] = both[:WIDE] + both[WIDE:] + mm(lhs[:WIDE, :], own_lo[:, n : n + 256])
+        for n in range(cols(i).start, virt, 256):
+            wide = slice(n, min(n + 256, virt))
+            both = mm(lhs[...], own_hi[:, wide])
+            part[i, :, wide] = both[:WIDE] + both[WIDE:] + mm(lhs[:WIDE, :], own_lo[:, wide])
         core_copy(i).start()
 
     def reduce_cores(i):
         core_copy(i).wait_recv()
-        red[i] = part[i, mine, :] + from_core[i]
+        red[i, :, cols(i)] = part[i, mine, cols(i)] + from_core[i, :, cols(i)]
 
         @pl.when(is_end)
         def _():
@@ -120,7 +129,7 @@
         @pl.when(is_mid)
         def _():
             end_copy(i).wait_recv()
-            red[i] = red[i] + from_end[i]
+            red[i, :, cols(i)] = red[i, :, cols(i)] + from_end[i, :, cols(i)]
             mid_copy(i).start()
 
     def amplitude(i):
@@ -129,9 +138,9 @@
             mid_copy(i).wait_recv()
             other = occ[(g, g_x, g_d)[i // nc]]
             first = (i % nc) * WIDE + core * half
-            col = vir_col[pl.ds(pl.multiple_of(first, half), half), :]
-            denom = (occ[g] - vir_row[...]) + (other - col)
-            amp[i, mine, :] = 1.3 * (red[i] + from_mid[i]) / denom
+            col = vir_col[pl.ds(pl.multiple_of(first, half), half), :][:, :1]
+            denom = (occ[g] - vir_row[:, cols(i).start :]) + (other - col)
+            amp[i, mine, cols(i)] = 1.3 * (red[i, :, cols(i)] + from_mid[i, :, cols(i)]) / denom
             back_copy(i).start()
             twin_copy(i).start()
 
@@ -144,41 +153,53 @@
     def density(i):
         for j in (i - 1, i):
             twin_copy(j).wait_recv()
-        high, low = split_two(amp[i - 1 : i + 1].reshape(2 * WIDE, virt))
-        amp_hi[...] = high
-        amp_lo[...] = low
+            pieces = [amp[j, :, cols(j)]]
+            if j < nc:
+                pieces = [amp[k, :, j * WIDE : (j + 1) * WIDE].T for k in range(j)] + pieces
+            high, low = split_two(jnp.concatenate(pieces, axis=1))
+            place = slice((j - i + 1) * WIDE, (j - i + 2) * WIDE)
+            amp_hi[place, :] = high
+            amp_lo[place, :] = low
 
         def add(m, carry):
             r = pl.ds(pl.multiple_of(m * tile, tile), tile)
             bh, bl = split_two(jnp.concatenate([chunk(i - 1, r), chunk(i, r)], axis=1))
-            out[r, :] += mm(bh, amp_hi[...]) + mm(bl, amp_hi[...]) + mm(bh, amp_lo[...])
+            value = total[r, :] + (mm(bh, amp_hi[...]) + mm(bl, amp_hi[...]) + mm(bh, amp_lo[...]))
+            if i < 3 * nc - 1:
+                total[r, :] = value
+            else:
+                for k in range(nc):
+                    out[pl.ds(m * (tile * nc) + k, tile, nc), :] = value[:, k * WIDE : (k + 1) * WIDE]
             return carry
 
         lax.fori_loop(0, rows // tile, add, 0)
 
-    order = list(range(nc)) + [nc]
-    for k in range(1, nc):
-        order += [nc + k, 2 * nc + k - 1]
-    order.append(3 * nc - 1)
-
-    forwarded = 0
-    for t in range(len(order) + 9):
-        if 0 <= t - 8 < len(order) and order[t - 8] % 2 == 1:
-            density(order[t - 8])
+    order, forward = [0], {}
+    for s in range(nc * SPLIT + 1):
+        if s < nc * SPLIT:
+            forward[s] = len(order)
+        if s % SPLIT == 1:
+            order.append(nc + s // SPLIT)
+        elif s >= SPLIT:
+            order.append(2 * nc + s // SPLIT - 1)
+        if s < nc - 1:
+            order.append(s + 1)
+
+    for t in range(len(order) + 8):
+        if 0 <= t - 7 < len(order) and order[t - 7] % 2 == 1:
+            density(order[t - 7])
         if 0 <= t - 6 < len(order):
             arrived(order[t - 6])
         if 0 <= t - 4 < len(order):
             amplitude(order[t - 4])
         if 0 <= t - 2 < len(order):
             reduce_line(order[t - 2])
+        for s in forward:
+            if forward[s] == t:
+                x_copy(s).wait_recv()
+                y_copy(s).start()
         if t < len(order):
             i = order[t]
-            if i >= nc and forwarded < nc * SPLIT:
-                last = (i - nc + 1) * SPLIT if i < 2 * nc else (i - 2 * nc + 1) * SPLIT + 1
-                while forwarded < min(last, nc * SPLIT):
-                    x_copy(forwarded).wait_recv()
-                    y_copy(forwarded).start()
-                    forwarded += 1
             if i >= 2 * nc:
                 for s in range((i - 2 * nc) * SPLIT, (i - 2 * nc + 1) * SPLIT):
                     y_copy(s).wait_recv()
@@ -213,11 +234,13 @@
     vmem = pl.BlockSpec(memory_space=pltpu.VMEM)
     result = pl.pallas_call(
         kernel,
-        out_shape=jax.ShapeDtypeStruct((rows, virt), f32),
-        in_specs=[vmem, pl.BlockSpec(memory_space=pltpu.SMEM), vmem, vmem],
+        out_shape=jax.ShapeDtypeStruct((rows * nc, WIDE), f32),
+        in_specs=[vmem, pl.BlockSpec(memory_space=pltpu.SMEM), vmem],
         out_specs=vmem,
         scratch_shapes=[
-            pltpu.VMEM((2 * nc, rows, WIDE), f32),
+            pltpu.VMEM((3 * nc, rows, WIDE), f32),
+            pltpu.VMEM((rows, virt), f32),
+            pltpu.VMEM((virt, WIDE), f32),
             pltpu.VMEM((rows, virt), bf16),
             pltpu.VMEM((rows, virt), bf16),
             pltpu.VMEM((items, WIDE, virt), f32),
@@ -238,7 +261,7 @@
         cost_estimate=pl.CostEstimate(
             flops=36 * rows * virt * virt, bytes_accessed=8 * rows * virt, transcendentals=0
         ),
-    )(factors.reshape(rows, virt), eps_occ, eps_vir.reshape(1, virt), eps_vir.reshape(virt, 1))
+    )(factors.reshape(rows * nc, WIDE), eps_occ, eps_vir)
     return result.reshape(rows, 1, virt)
 
 

time: 147 us -> 128 us (0.87)
  Pallas kernels: 133 us -> 122 us
  local copies, waits for them, and re-layouts: 13.4 us -> 5.71 us
    pallas_call x1, Pallas kernels: 133 us -> 122 us  [line_body(): pl.pallas_call(kernel, out_shape=jax.ShapeDtypeStruct((rows * nc, WIDE),...]
    reshape x3 -> x0, local copies, waits for them, and re-layouts: 9.67 us -> none  [the longest x1 6.79 us: line_body(): return result.reshape(rows, 1, virt)]
    unnamed x1, local copies, waits for them, and re-layouts: 3.75 us -> 5.71 us
where the time goes in v2:
time: 128 us
  Pallas kernels  122 us (95%)
  local copies, waits for them, and re-layouts  5.71 us (4%)
    pallas_call x1, Pallas kernels, line_body(): pl.pallas_call(kernel, out_shape=jax.ShapeDtypeStruct((rows * nc, WIDE),...  122 us
    unnamed x1, local copies, waits for them, and re-layouts  5.71 us

profile of v2, /device:TPU:1, one launch (start us, length us, event | category | flops | bytes accessed | tf_op | source)
XLA Modules:
  0.0 127.7 jit_solution(8920958022804288946)
XLA Ops:
  0.0 122.0 %shard_map.37 = f32[6144,128]{1,0:T(8,128)} custom-call(f32[6144,128]{1,0:T(8,128)} %bitcast.3, f32[4]{0:T(128)} %occ.1, f32[768]{0:T(1024)} %vir.1), custom_call_target="tpu_custom_call" | custom-call | flops 21743271936 | bytes 6291456 | tf_op jit(solution)/shard_map/pallas_call | solution.py:235
  122.0 5.7 %copy.6 = f32[1024,1,768]{2,1,0:T(1,128)} copy(f32[1024,1,768]{2,1,0:T(1,128)} %bitcast.2) | data formatting | bytes 6291456

commit v3 on v2

--- a/solution.py
+++ b/solution.py
@@ -24,7 +24,7 @@
 
 def kernel(
     given, occ, vir, out,
-    near, total, vir_col, own_hi, own_lo, part, from_core, from_end, from_mid, red, amp, lhs, amp_hi, amp_lo,
+    near, total, vir_col, own_hi, own_lo, part, from_core, from_end, from_mid, red, amp, lhs, amp_three,
     x_send, x_recv, y_send, y_recv, c_send, c_recv, e_send, e_recv, m_send, m_recv, b_send, b_recv, t_send, t_recv,
 ):
     rows, virt = total.shape
@@ -140,7 +140,7 @@
             first = (i % nc) * WIDE + core * half
             col = vir_col[pl.ds(pl.multiple_of(first, half), half), :][:, :1]
             denom = (occ[g] - vir_row[:, cols(i).start :]) + (other - col)
-            amp[i, mine, cols(i)] = 1.3 * (red[i, :, cols(i)] + from_mid[i, :, cols(i)]) / denom
+            amp[i, mine, cols(i)] = (red[i, :, cols(i)] + from_mid[i, :, cols(i)]) / denom
             back_copy(i).start()
             twin_copy(i).start()
 
@@ -158,13 +158,15 @@
                 pieces = [amp[k, :, j * WIDE : (j + 1) * WIDE].T for k in range(j)] + pieces
             high, low = split_two(jnp.concatenate(pieces, axis=1))
             place = slice((j - i + 1) * WIDE, (j - i + 2) * WIDE)
-            amp_hi[place, :] = high
-            amp_lo[place, :] = low
+            amp_three[0, place, :] = high
+            amp_three[1, place, :] = high
+            amp_three[2, place, :] = low
 
         def add(m, carry):
             r = pl.ds(pl.multiple_of(m * tile, tile), tile)
             bh, bl = split_two(jnp.concatenate([chunk(i - 1, r), chunk(i, r)], axis=1))
-            value = total[r, :] + (mm(bh, amp_hi[...]) + mm(bl, amp_hi[...]) + mm(bh, amp_lo[...]))
+            three = amp_three[...].reshape(6 * WIDE, virt)
+            value = total[r, :] + mm(jnp.concatenate([bh, bl, bh], axis=1), three)
             if i < 3 * nc - 1:
                 total[r, :] = value
             else:
@@ -185,26 +187,29 @@
         if s < nc - 1:
             order.append(s + 1)
 
-    for t in range(len(order) + 8):
-        if 0 <= t - 7 < len(order) and order[t - 7] % 2 == 1:
-            density(order[t - 7])
-        if 0 <= t - 6 < len(order):
-            arrived(order[t - 6])
-        if 0 <= t - 4 < len(order):
-            amplitude(order[t - 4])
-        if 0 <= t - 2 < len(order):
-            reduce_line(order[t - 2])
+    def late(stage, t):
+        if 0 <= t < len(order) and (stage is not density or order[t] % 2 == 1):
+            stage(order[t])
+
+    for t, i in enumerate(order):
+        late(arrived, t - 6)
+        late(reduce_line, t - 2)
         for s in forward:
             if forward[s] == t:
                 x_copy(s).wait_recv()
                 y_copy(s).start()
-        if t < len(order):
-            i = order[t]
-            if i >= 2 * nc:
-                for s in range((i - 2 * nc) * SPLIT, (i - 2 * nc + 1) * SPLIT):
-                    y_copy(s).wait_recv()
-            integral(i)
-            reduce_cores(i)
+        if i >= 2 * nc:
+            for s in range((i - 2 * nc) * SPLIT, (i - 2 * nc + 1) * SPLIT):
+                y_copy(s).wait_recv()
+        integral(i)
+        late(amplitude, t - 4)
+        late(density, t - 7)
+        reduce_cores(i)
+    for t in range(len(order), len(order) + 8):
+        late(density, t - 7)
+        late(arrived, t - 6)
+        late(amplitude, t - 4)
+        late(reduce_line, t - 2)
 
     for s in range(nc * SPLIT):
         x_copy(s).wait_send()
@@ -250,8 +255,7 @@
             pltpu.VMEM((items, WIDE // 2, virt), f32),
             pltpu.VMEM((items, WIDE, virt), f32),
             pltpu.VMEM((2 * WIDE, rows), bf16),
-            pltpu.VMEM((2 * WIDE, virt), bf16),
-            pltpu.VMEM((2 * WIDE, virt), bf16),
+            pltpu.VMEM((3, 2 * WIDE, virt), bf16),
         ]
         + [dma((nc * SPLIT,))] * 4
         + [dma((items,))] * 10,
@@ -262,7 +266,7 @@
             flops=36 * rows * virt * virt, bytes_accessed=8 * rows * virt, transcendentals=0
         ),
     )(factors.reshape(rows * nc, WIDE), eps_occ, eps_vir)
-    return result.reshape(rows, 1, virt)
+    return (1.3 * result).reshape(rows, 1, virt)
 
 
 def passed_along(value, axis, steps):

time: 128 us -> 130 us (1.016)
  local copies, waits for them, and re-layouts: 5.71 us -> 0 us
  Pallas kernels: 122 us -> 126 us
  other arithmetic: 0 us -> 3.82 us
    unnamed x1 -> x0, local copies, waits for them, and re-layouts: 5.71 us -> none
    pallas_call x1, Pallas kernels: 122 us -> 126 us  [line_body(): pl.pallas_call(kernel, out_shape=jax.ShapeDtypeStruct((rows * nc, WIDE),...]
    mul x0 -> x1, other arithmetic: none -> 3.82 us  [line_body(): return (1.3 * result).reshape(rows, 1, virt)]
where the time goes in v3:
time: 130 us
  Pallas kernels  126 us (97%)
  other arithmetic  3.82 us (3%)
    pallas_call x1, Pallas kernels, line_body(): pl.pallas_call(kernel, out_shape=jax.ShapeDtypeStruct((rows * nc, WIDE),...  126 us
    mul x1, other arithmetic, line_body(): return (1.3 * result).reshape(rows, 1, virt)  3.82 us

profile of v3, /device:TPU:1, one launch (start us, length us, event | category | flops | bytes accessed | tf_op | source)
XLA Modules:
  0.0 130.2 jit_solution(8904018964582731949)
XLA Ops:
  0.0 126.4 %shard_map.37 = f32[6144,128]{1,0:T(8,128)} custom-call(f32[6144,128]{1,0:T(8,128)} %bitcast.2, f32[4]{0:T(128)} %occ.1, f32[768]{0:T(1024)} %vir.1), custom_call_target="tpu_custom_call" | custom-call | flops 21743271936 | bytes 6291456 | tf_op jit(solution)/shard_map/pallas_call | solution.py:240
  126.4 3.8 %broadcast_multiply_fusion = f32[6144,128]{1,0:T(8,128)} fusion(f32[6144,128]{1,0:T(8,128)} %shard_map.37), kind=kLoop, calls=%fused_computation | loop fusion | flops 786432 | bytes 6291456 | tf_op jit(solution)/shard_map/mul | solution.py:269

commit v4 on v3

--- a/solution.py
+++ b/solution.py
@@ -191,8 +191,11 @@
         if 0 <= t < len(order) and (stage is not density or order[t] % 2 == 1):
             stage(order[t])
 
+    count = len(order)
     for t, i in enumerate(order):
+        late(density, t - 7)
         late(arrived, t - 6)
+        late(amplitude, t - 4)
         late(reduce_line, t - 2)
         for s in forward:
             if forward[s] == t:
@@ -202,14 +205,26 @@
             for s in range((i - 2 * nc) * SPLIT, (i - 2 * nc + 1) * SPLIT):
                 y_copy(s).wait_recv()
         integral(i)
-        late(amplitude, t - 4)
-        late(density, t - 7)
         reduce_cores(i)
-    for t in range(len(order), len(order) + 8):
-        late(density, t - 7)
-        late(arrived, t - 6)
-        late(amplitude, t - 4)
-        late(reduce_line, t - 2)
+    late(reduce_line, count - 2)
+    late(amplitude, count - 4)
+    late(density, count - 7)
+    late(arrived, count - 6)
+    late(amplitude, count - 3)
+    late(density, count - 6)
+    late(reduce_line, count - 1)
+    late(amplitude, count - 2)
+    late(arrived, count - 5)
+    late(density, count - 5)
+    late(arrived, count - 4)
+    late(arrived, count - 3)
+    late(amplitude, count - 1)
+    late(density, count - 4)
+    late(density, count - 3)
+    late(arrived, count - 2)
+    late(density, count - 2)
+    late(arrived, count - 1)
+    late(density, count - 1)
 
     for s in range(nc * SPLIT):
         x_copy(s).wait_send()

time: 130 us -> 126 us (0.969)
  Pallas kernels: 126 us -> 122 us
    pallas_call x1, Pallas kernels: 126 us -> 122 us  [line_body(): pl.pallas_call(kernel, out_shape=jax.ShapeDtypeStruct((rows * nc, WIDE),...]
where the time goes in v4:
time: 126 us; the launch traced here: 125 us
  Pallas kernels  122 us (97%)
  other arithmetic  3.82 us (3%)
    pallas_call x1, Pallas kernels, line_body(): pl.pallas_call(kernel, out_shape=jax.ShapeDtypeStruct((rows * nc, WIDE),...  122 us
    mul x1, other arithmetic, line_body(): return (1.3 * result).reshape(rows, 1, virt)  3.82 us

profile of v4, /device:TPU:1, one launch (start us, length us, event | category | flops | bytes accessed | tf_op | source)
XLA Modules:
  0.0 125.5 jit_solution(10959953420318109866)
XLA Ops:
  0.0 121.6 %shard_map.37 = f32[6144,128]{1,0:T(8,128)} custom-call(f32[6144,128]{1,0:T(8,128)} %bitcast.2, f32[4]{0:T(128)} %occ.1, f32[768]{0:T(1024)} %vir.1), custom_call_target="tpu_custom_call" | custom-call | flops 21743271936 | bytes 6291456 | tf_op jit(solution)/shard_map/pallas_call | solution.py:255
  121.6 3.8 %broadcast_multiply_fusion = f32[6144,128]{1,0:T(8,128)} fusion(f32[6144,128]{1,0:T(8,128)} %shard_map.37), kind=kLoop, calls=%fused_computation | loop fusion | flops 786432 | bytes 6291456 | tf_op jit(solution)/shard_map/mul | solution.py:284

commit v5 on v4

--- a/solution.py
+++ b/solution.py
@@ -193,14 +193,14 @@
 
     count = len(order)
     for t, i in enumerate(order):
+        for s in forward:
+            if max(s + 1, forward[s] - 1 - (3 < s < 8)) == t:
+                x_copy(s).wait_recv()
+                y_copy(s).start()
         late(density, t - 7)
         late(arrived, t - 6)
         late(amplitude, t - 4)
         late(reduce_line, t - 2)
-        for s in forward:
-            if forward[s] == t:
-                x_copy(s).wait_recv()
-                y_copy(s).start()
         if i >= 2 * nc:
             for s in range((i - 2 * nc) * SPLIT, (i - 2 * nc + 1) * SPLIT):
                 y_copy(s).wait_recv()

time: 126 us -> 121 us (0.960)
  Pallas kernels: 122 us -> 116 us
    pallas_call x1, Pallas kernels: 122 us -> 116 us  [line_body(): pl.pallas_call(kernel, out_shape=jax.ShapeDtypeStruct((rows * nc, WIDE),...]
where the time goes in v5:
time: 121 us; the launch traced here: 120 us
  Pallas kernels  116 us (96%)
  other arithmetic  3.82 us (3%)
    pallas_call x1, Pallas kernels, line_body(): pl.pallas_call(kernel, out_shape=jax.ShapeDtypeStruct((rows * nc, WIDE),...  116 us
    mul x1, other arithmetic, line_body(): return (1.3 * result).reshape(rows, 1, virt)  3.82 us

profile of v5, /device:TPU:1, one launch (start us, length us, event | category | flops | bytes accessed | tf_op | source)
XLA Modules:
  0.0 119.5 jit_solution(7201463713300164344)
XLA Ops:
  0.0 115.7 %shard_map.37 = f32[6144,128]{1,0:T(8,128)} custom-call(f32[6144,128]{1,0:T(8,128)} %bitcast.2, f32[4]{0:T(128)} %occ.1, f32[768]{0:T(1024)} %vir.1), custom_call_target="tpu_custom_call" | custom-call | flops 21743271936 | bytes 6291456 | tf_op jit(solution)/shard_map/pallas_call | solution.py:255
  115.7 3.8 %broadcast_multiply_fusion = f32[6144,128]{1,0:T(8,128)} fusion(f32[6144,128]{1,0:T(8,128)} %shard_map.37), kind=kLoop, calls=%fused_computation | loop fusion | flops 786432 | bytes 6291456 | tf_op jit(solution)/shard_map/mul | solution.py:284
